TPU v7x, 256 devices: a whole 4x4x8 slice. The times are simulated.
256 devices in a mesh: dp: 16 (over y_lo, x, core), seq: 16 (over z, y_hi).
Axes of the slice: x: 4, y: 4 (y_hi: 2, y_lo: 2; y = y_hi * 2 + y_lo), z: 8, core: 2. Of those that a mesh axis runs over, the one named last changes fastest.
Arguments:
- primal: bfloat16 [16, 2048, 3, 4096], P('dp', 'seq'), as said below
- tangent: bfloat16 [16, 2048, 3, 4096], P('dp', 'seq'), may hold values from -6 to 6
- cotangent: bfloat16 [16, 2048, 2560], P('dp', 'seq'), may hold values from -6 to 6
Outputs:
- attended: bfloat16 [16, 2048, 4096], P('dp', 'seq')
- attended_tangent: bfloat16 [16, 2048, 4096], P('dp', 'seq')
- weight_grad: float32 [2560, 4096], P('dp', 'seq')
Inputs may be any that keep to these rules, and one draw needn't show every extreme that they name: `primal`: slots 0, 1, 2 of the third dimension are queries, keys and values.
All inputs are finite; a program needn't handle non-finite values.
Results may differ from a plain program's by a relative error of at most 0.005.
Values may be sent and summed in bfloat16 or wider, within the bound.
A program may use at most 128 MiB of HBM per device.

v0:
```python
import jax
import jax.numpy as jnp
from jax import lax
from jax.sharding import PartitionSpec as P

HEAD_DIM = 128


def block_jvp(query_block, dquery_block, keys, dkeys, values, dvalues):
    scale = 1.0 / HEAD_DIM**0.5
    scores = (
        jnp.einsum("qhd,khd->hqk", query_block, keys, preferred_element_type=jnp.float32) * scale
    )
    top = jnp.max(scores, axis=-1, keepdims=True)
    expo = jnp.exp(scores - top)
    probs = expo / jnp.sum(expo, axis=-1, keepdims=True)
    probs_low = probs.astype(jnp.bfloat16)
    out = jnp.einsum("hqk,khd->qhd", probs_low, values, preferred_element_type=jnp.float32)
    dscores = jnp.einsum("qhd,khd->hqk", dquery_block, keys, preferred_element_type=jnp.float32)
    dscores = (
        dscores + jnp.einsum("qhd,khd->hqk", query_block, dkeys, preferred_element_type=jnp.float32)
    ) * scale
    centre = jnp.sum(probs * dscores, axis=-1, keepdims=True)
    dprobs = (probs * (dscores - centre)).astype(jnp.bfloat16)
    dout = jnp.einsum("hqk,khd->qhd", probs_low, dvalues, preferred_element_type=jnp.float32)
    dout = dout + jnp.einsum("hqk,khd->qhd", dprobs, values, preferred_element_type=jnp.float32)
    return (out.astype(jnp.bfloat16), dout.astype(jnp.bfloat16))


def body(primal, tangent, cotangent):
    prim_heads, tang_heads = (
        lax.all_to_all(primal, "seq", split_axis=3, concat_axis=1, tiled=True),
        lax.all_to_all(tangent, "seq", split_axis=3, concat_axis=1, tiled=True),
    )
    seq_len = prim_heads.shape[1]
    local_width = prim_heads.shape[3]
    head_count = local_width // HEAD_DIM
    prim_heads = prim_heads[0].reshape(seq_len, 3, head_count, HEAD_DIM)
    tang_heads = tang_heads[0].reshape(seq_len, 3, head_count, HEAD_DIM)
    keys, values = (prim_heads[:, 1], prim_heads[:, 2])
    dkeys, dvalues = (tang_heads[:, 1], tang_heads[:, 2])
    block = min(512, seq_len)
    queries = prim_heads[:, 0].reshape(seq_len // block, block, head_count, HEAD_DIM)
    dqueries = tang_heads[:, 0].reshape(seq_len // block, block, head_count, HEAD_DIM)

    def one_block(pair):
        return block_jvp(pair[0], pair[1], keys, dkeys, values, dvalues)

    outs, douts = lax.map(one_block, (queries, dqueries))
    outs = outs.reshape(1, seq_len, local_width)
    douts = douts.reshape(1, seq_len, local_width)
    attended, attended_tangent = (
        lax.all_to_all(outs, "seq", split_axis=1, concat_axis=2, tiled=True),
        lax.all_to_all(douts, "seq", split_axis=1, concat_axis=2, tiled=True),
    )
    full_cot = lax.all_gather(cotangent, "seq", axis=1, tiled=True)[0]
    heads_out = outs[0]
    term = lax.dot_general(
        full_cot, heads_out, (((0,), (0,)), ((), ())), preferred_element_type=jnp.float32
    )
    weight_grad = lax.psum_scatter(term, "dp", scatter_dimension=0, tiled=True)
    return (attended, attended_tangent, weight_grad)


def solution(mesh):
    return jax.shard_map(
        body,
        mesh=mesh,
        in_specs=(P("dp", "seq", None, None), P("dp", "seq", None, None), P("dp", "seq", None)),
        out_specs=(P("dp", "seq", None), P("dp", "seq", None), P("dp", "seq")),
        check_vma=False,
    )
```

profile of v0, /device:TPU:6, one launch (start us, length us, event | category | flops | bytes accessed | tf_op | source)
XLA Modules:
  0.0 478.7 jit_solution(12705735730795649485)
XLA Ops:
  7.2 7.3 %copy.42 = bf16[1,128,3,4096]{1,2,0,3:T(4,128)(2,1)} copy(bf16[1,128,3,4096]{3,1,2,0:T(8,128)(2,1)} %param.6) | data formatting | bytes 6291456 | tf_op args[1]
  14.5 11.3 %all-to-all-start.1 = ((bf16[1,128,3,4096]{1,2,0,3:T(4,128)(2,1)}), bf16[1,128,3,4096]{1,2,0,3:T(4,128)(2,1)}, u32[]{:S(2)}, u32[]{:S(2)}) async-start(bf16[1,128,3,4096]{1,2,0,3:T(4,128)(2,1)} %copy.42), calls=%async_computation.1 | async-start | bytes 8388608 | tf_op jit(solution)/shard_map/all_to_all | solution.py:33
  25.8 4.8 copy.39
  30.5 94.0 %all-to-all-done.1 = bf16[1,128,3,4096]{1,2,0,3:T(4,128)(2,1)} async-done(((bf16[1,128,3,4096]{1,2,0,3:T(4,128)(2,1)}), bf16[1,128,3,4096]{1,2,0,3:T(4,128)(2,1)}, u32[]{:S(2)}, u32[]{:S(2)}) %all-to-all-start.1) | async-done | bytes 3145760 | tf_op jit(solution)/shard_map/all_to_all | solution.py:33
  124.6 5.2 %all-to-all-start = ((bf16[1,128,3,4096]{1,2,0,3:T(4,128)(2,1)}), bf16[1,128,3,4096]{1,2,0,3:T(4,128)(2,1)}, u32[]{:S(2)}, u32[]{:S(2)}) async-start(bf16[1,128,3,4096]{1,2,0,3:T(4,128)(2,1)} %copy.39), calls=%async_computation | async-start | bytes 8388608 | tf_op jit(solution)/shard_map/all_to_all | solution.py:32
  130.6 4.8 copy.80
  143.5 105.6 %all-to-all-done = bf16[1,128,3,4096]{1,2,0,3:T(4,128)(2,1)} async-done(((bf16[1,128,3,4096]{1,2,0,3:T(4,128)(2,1)}), bf16[1,128,3,4096]{1,2,0,3:T(4,128)(2,1)}, u32[]{:S(2)}, u32[]{:S(2)}) %all-to-all-start) | async-done | bytes 3145760 | tf_op jit(solution)/shard_map/all_to_all | solution.py:32
  249.1 4.8 copy.81
  270.1 99.2 %while.12 = (s32[]{:T(128)}, bf16[4,512,2,128]{3,2,1,0:T(2,128)(2,1)S(1)}, bf16[4,512,2,128]{3,2,1,0:T(2,128)(2,1)}, bf16[4,512,2,128]{3,1,0,2:T(8,128)(2,1)}, b...) while((s32[]{:T(128)}, ...), condition=%wide.region_4.5_spmd, body=%wide.region_0.4_spmd.sunk | while | flops 3255174144 | bytes 131365072 | solution.py:49
  270.1 6.9 %fusion.95 = (f32[2,512]{1,0:T(2,128)S(1)}, f32[2,512,2048]{2,1,0:T(8,128)}) fusion(bf16[2048,2,128]{2,0,1:T(8,128)(2,1)S(1)} %get-tuple-element.213, bf16[4,512,2,128]{3,1,0,2:T(8,128)(2,1)} %get-tuple-element.212, s32[]{:T(128)} %get-tuple-element.199), kind=kOutput, calls=%fused_computation.49.clone.1 | convolution fusion | flops 543164416 | bytes 9703936 | tf_op jit(solution)/shard_map/while/body/eval_jaxpr/sub | solution.py:15
  280.7 5.5 %multiply_reduce_fusion.3 = (f32[2,512]{1,0:T(2,128)S(1)}, f32[2,512,2048]{2,1,0:T(8,128)}) fusion(f32[2,512,2048]{2,1,0:T(8,128)S(1)} %copy-done.7, f32[2,512]{1,0:T(2,128)S(1)} %get-tuple-element.184, f32[2,512,2048]{2,1,0:T(8,128)S(1)} %fusion.96, bf16[2048,2,128]{2,0,1:T(8,128)(2,1)S(1)} %copy-done.6, ...), kind=kOutput, calls=%fused_computation.2.clone.1 | convolution fusion | flops 547355648 | bytes 26485248 | tf_op jit(solution)/shard_map/while/body/eval_jaxpr/qhd,khd->hqk/dot_general | solution.py:21
  294.8 6.9 %fusion.95 = (f32[2,512]{1,0:T(2,128)S(1)}, f32[2,512,2048]{2,1,0:T(8,128)}) fusion(bf16[2048,2,128]{2,0,1:T(8,128)(2,1)S(1)} %get-tuple-element.213, bf16[4,512,2,128]{3,1,0,2:T(8,128)(2,1)} %get-tuple-element.212, s32[]{:T(128)} %get-tuple-element.199), kind=kOutput, calls=%fused_computation.49.clone.1 | convolution fusion | flops 543164416 | bytes 9703936 | tf_op jit(solution)/shard_map/while/body/eval_jaxpr/sub | solution.py:15
  305.5 5.5 %multiply_reduce_fusion.3 = (f32[2,512]{1,0:T(2,128)S(1)}, f32[2,512,2048]{2,1,0:T(8,128)}) fusion(f32[2,512,2048]{2,1,0:T(8,128)S(1)} %copy-done.7, f32[2,512]{1,0:T(2,128)S(1)} %get-tuple-element.184, f32[2,512,2048]{2,1,0:T(8,128)S(1)} %fusion.96, bf16[2048,2,128]{2,0,1:T(8,128)(2,1)S(1)} %copy-done.6, ...), kind=kOutput, calls=%fused_computation.2.clone.1 | convolution fusion | flops 547355648 | bytes 26485248 | tf_op jit(solution)/shard_map/while/body/eval_jaxpr/qhd,khd->hqk/dot_general | solution.py:21
  319.6 6.9 %fusion.95 = (f32[2,512]{1,0:T(2,128)S(1)}, f32[2,512,2048]{2,1,0:T(8,128)}) fusion(bf16[2048,2,128]{2,0,1:T(8,128)(2,1)S(1)} %get-tuple-element.213, bf16[4,512,2,128]{3,1,0,2:T(8,128)(2,1)} %get-tuple-element.212, s32[]{:T(128)} %get-tuple-element.199), kind=kOutput, calls=%fused_computation.49.clone.1 | convolution fusion | flops 543164416 | bytes 9703936 | tf_op jit(solution)/shard_map/while/body/eval_jaxpr/sub | solution.py:15
  330.3 5.6 %multiply_reduce_fusion.3 = (f32[2,512]{1,0:T(2,128)S(1)}, f32[2,512,2048]{2,1,0:T(8,128)}) fusion(f32[2,512,2048]{2,1,0:T(8,128)S(1)} %copy-done.7, f32[2,512]{1,0:T(2,128)S(1)} %get-tuple-element.184, f32[2,512,2048]{2,1,0:T(8,128)S(1)} %fusion.96, bf16[2048,2,128]{2,0,1:T(8,128)(2,1)S(1)} %copy-done.6, ...), kind=kOutput, calls=%fused_computation.2.clone.1 | convolution fusion | flops 547355648 | bytes 26485248 | tf_op jit(solution)/shard_map/while/body/eval_jaxpr/qhd,khd->hqk/dot_general | solution.py:21
  344.5 6.9 %fusion.95 = (f32[2,512]{1,0:T(2,128)S(1)}, f32[2,512,2048]{2,1,0:T(8,128)}) fusion(bf16[2048,2,128]{2,0,1:T(8,128)(2,1)S(1)} %get-tuple-element.213, bf16[4,512,2,128]{3,1,0,2:T(8,128)(2,1)} %get-tuple-element.212, s32[]{:T(128)} %get-tuple-element.199), kind=kOutput, calls=%fused_computation.49.clone.1 | convolution fusion | flops 543164416 | bytes 9703936 | tf_op jit(solution)/shard_map/while/body/eval_jaxpr/sub | solution.py:15
  355.2 5.5 %multiply_reduce_fusion.3 = (f32[2,512]{1,0:T(2,128)S(1)}, f32[2,512,2048]{2,1,0:T(8,128)}) fusion(f32[2,512,2048]{2,1,0:T(8,128)S(1)} %copy-done.7, f32[2,512]{1,0:T(2,128)S(1)} %get-tuple-element.184, f32[2,512,2048]{2,1,0:T(8,128)S(1)} %fusion.96, bf16[2048,2,128]{2,0,1:T(8,128)(2,1)S(1)} %copy-done.6, ...), kind=kOutput, calls=%fused_computation.2.clone.1 | convolution fusion | flops 547355648 | bytes 26485248 | tf_op jit(solution)/shard_map/while/body/eval_jaxpr/qhd,khd->hqk/dot_general | solution.py:21
  370.2 5.9 %fusion.53 = f32[2560,256]{0,1:T(8,128)S(1)} fusion(bf16[1,2048,2560]{2,1,0:T(8,128)(2,1)} %all-gather.2.cloned.1.call-done, bf16[256,8,2,128]{3,2,1,0:T(2,128)(2,1)} %bitcast.118), kind=kOutput, calls=%fused_computation.40 | convolution fusion | flops 2684354560 | bytes 14155776 | tf_op jit(solution)/shard_map/dot_general | solution.py:58
  378.3 6.4 %reshape.19 = bf16[1,2048,256]{2,0,1:T(2,128)(2,1)S(1)} reshape(bf16[4,512,2,128]{3,2,1,0:T(2,128)(2,1)} %copy-done.1) | data formatting | bytes 2097152 | tf_op jit(solution)/shard_map/reshape | solution.py:50
  385.2 10.7 %reduce = bf16[2048,256]{1,0:T(8,128)(2,1)S(1)} reduce(bf16[2048,1,256]{2,1,0:T(2,128)(2,1)S(1)} %bitcast.116, bf16[]{:T(256)} %broadcast.18), dimensions={1}, to_apply=%bitcast.71.reduce_sub_computation | reduce | bytes 2097154
  401.7 6.4 %reshape.20 = bf16[1,2048,256]{2,0,1:T(2,128)(2,1)S(1)} reshape(bf16[4,512,2,128]{3,2,1,0:T(2,128)(2,1)} %get-tuple-element.52) | data formatting | bytes 2097152 | tf_op jit(solution)/shard_map/reshape | solution.py:51
  408.1 11.5 %reduce.1 = bf16[2048,256]{1,0:T(8,128)(2,1)} reduce(bf16[2048,1,256]{2,1,0:T(2,128)(2,1)S(1)} %bitcast.117, bf16[]{:T(256)} %broadcast.18), dimensions={1}, to_apply=%bitcast.73.reduce_sub_computation | reduce | bytes 2097154
  421.8 10.0 %all-to-all-done.2 = bf16[16,2,16384]{2,1,0:T(2,128)(2,1)S(1)} async-done(((bf16[16,2,16384]{2,1,0:T(2,128)(2,1)}), bf16[16,2,16384]{2,1,0:T(2,128)(2,1)S(1)}, u32[]{:S(2)}, u32[]{:S(2)}) %all-to-all-start.2) | async-done | bytes 1048608 | tf_op jit(solution)/shard_map/all_to_all | solution.py:53
  439.4 25.9 %all-to-all-done.3 = bf16[16,2,16384]{2,1,0:T(2,128)(2,1)} async-done(((bf16[16,2,16384]{2,1,0:T(2,128)(2,1)}), bf16[16,2,16384]{2,1,0:T(2,128)(2,1)}, u32[]{:S(2)}, u32[]{:S(2)}) %all-to-all-start.3) | async-done | bytes 1048608 | tf_op jit(solution)/shard_map/all_to_all | solution.py:54
  (92 shorter events, 100.3 us)
Async XLA Ops:
  7.2 18.6 %copy-start.3 = (bf16[1,128,3,4096]{3,1,2,0:T(8,128)(2,1)S(1)}, bf16[1,128,3,4096]{3,1,2,0:T(8,128)(2,1)}, u32[]{:S(2)}) copy-start(bf16[1,128,3,4096]{3,1,2,0:T(8,128)(2,1)} %param.5) | copy-start | bytes 9437188
  14.5 110.1 %all-to-all-start.1 = ((bf16[1,128,3,4096]{1,2,0,3:T(4,128)(2,1)}), bf16[1,128,3,4096]{1,2,0,3:T(4,128)(2,1)}, u32[]{:S(2)}, u32[]{:S(2)}) async-start(bf16[1,128,3,4096]{1,2,0,3:T(4,128)(2,1)} %copy.42), calls=%async_computation.1 | async-start | bytes 8388608 | tf_op jit(solution)/shard_map/all_to_all | solution.py:33
  124.6 124.5 %all-to-all-start = ((bf16[1,128,3,4096]{1,2,0,3:T(4,128)(2,1)}), bf16[1,128,3,4096]{1,2,0,3:T(4,128)(2,1)}, u32[]{:S(2)}, u32[]{:S(2)}) async-start(bf16[1,128,3,4096]{1,2,0,3:T(4,128)(2,1)} %copy.39), calls=%async_computation | async-start | bytes 8388608 | tf_op jit(solution)/shard_map/all_to_all | solution.py:32
  129.8 239.5 %all-gather.2.cloned.1.call-start = ((), (), s32[]{:S(2)}) async-start(), calls=%async_computation.5 | async-start | bytes 11141120 | tf_op jit(solution)/shard_map/all_gather | solution.py:56
  130.5 341.3 %reduce-scatter.4.cloned.1.call-start = ((), (), s32[]{:S(2)}) async-start(), calls=%async_computation.6 | async-start | bytes 2785280
  257.2 11.5 %copy-start.2 = (bf16[2048,2,128]{0,2,1:T(8,128)(2,1)S(1)}, bf16[2048,2,128]{0,2,1:T(8,128)(2,1)}, u32[]{:S(2)}) copy-start(bf16[2048,2,128]{0,2,1:T(8,128)(2,1)} %get-tuple-element.116) | copy-start | bytes 3145732
  257.2 12.8 %copy-start = (bf16[4,512,2,128]{3,2,1,0:T(2,128)(2,1)S(1)}, bf16[4,512,2,128]{3,2,1,0:T(2,128)(2,1)}, u32[]{:S(2)}) copy-start(bf16[4,512,2,128]{3,2,1,0:T(2,128)(2,1)} %custom-call) | copy-start | bytes 3145732
  276.9 2.4 copy-start.6
  276.9 3.8 copy-start.7
  280.7 5.5 %copy-start.4 = (bf16[2048,2,128]{2,0,1:T(8,128)(2,1)S(1)}, bf16[2048,2,128]{2,0,1:T(8,128)(2,1)}, u32[]{:S(2)}) copy-start(bf16[2048,2,128]{2,0,1:T(8,128)(2,1)} %get-tuple-element.214) | copy-start | bytes 3145732 | tf_op jit(solution)/shard_map/while
  286.2 4.5 copy-start.5
  301.6 2.4 copy-start.6
  301.6 3.9 copy-start.7
  305.5 5.5 %copy-start.4 = (bf16[2048,2,128]{2,0,1:T(8,128)(2,1)S(1)}, bf16[2048,2,128]{2,0,1:T(8,128)(2,1)}, u32[]{:S(2)}) copy-start(bf16[2048,2,128]{2,0,1:T(8,128)(2,1)} %get-tuple-element.214) | copy-start | bytes 3145732 | tf_op jit(solution)/shard_map/while
  311.0 4.5 copy-start.5
  326.4 2.4 copy-start.6
  326.4 3.9 copy-start.7
  330.3 5.6 %copy-start.4 = (bf16[2048,2,128]{2,0,1:T(8,128)(2,1)S(1)}, bf16[2048,2,128]{2,0,1:T(8,128)(2,1)}, u32[]{:S(2)}) copy-start(bf16[2048,2,128]{2,0,1:T(8,128)(2,1)} %get-tuple-element.214) | copy-start | bytes 3145732 | tf_op jit(solution)/shard_map/while
  335.9 4.6 copy-start.5
  351.4 3.8 copy-start.7
  355.2 5.5 %copy-start.4 = (bf16[2048,2,128]{2,0,1:T(8,128)(2,1)S(1)}, bf16[2048,2,128]{2,0,1:T(8,128)(2,1)}, u32[]{:S(2)}) copy-start(bf16[2048,2,128]{2,0,1:T(8,128)(2,1)} %get-tuple-element.214) | copy-start | bytes 3145732 | tf_op jit(solution)/shard_map/while
  360.7 4.5 copy-start.5
  397.1 34.7 %all-to-all-start.2 = ((bf16[16,2,16384]{2,1,0:T(2,128)(2,1)}), bf16[16,2,16384]{2,1,0:T(2,128)(2,1)S(1)}, u32[]{:S(2)}, u32[]{:S(2)}) async-start(bf16[16,2,16384]{2,1,0:T(2,128)(2,1)} %reshape.23), calls=%async_computation.2 | async-start | bytes 2097152 | tf_op jit(solution)/shard_map/all_to_all | solution.py:53
  431.8 33.6 %all-to-all-start.3 = ((bf16[16,2,16384]{2,1,0:T(2,128)(2,1)}), bf16[16,2,16384]{2,1,0:T(2,128)(2,1)}, u32[]{:S(2)}, u32[]{:S(2)}) async-start(bf16[16,2,16384]{2,1,0:T(2,128)(2,1)} %reshape.25), calls=%async_computation.3 | async-start | bytes 2097152 | tf_op jit(solution)/shard_map/all_to_all | solution.py:54
  (2 other events, 3.3 us)
Sparse Core Ops, SparseCore 0:
  133.2 223.3 all-gather.1
  378.5 61.9 reduce-scatter.3
where the time goes:
time: 480 us; the launch traced here: 479 us
  waiting for transfers between devices  236 us (49%)
  matrix products  94.1 us (20%)
  local copies, waits for them, and re-layouts  86.2 us (18%)
  starting transfers between devices  25.6 us (5%)
  other arithmetic  22.3 us (5%)
  between operations  14.2 us (3%)
    all_to_all x1, waiting for transfers between devices, body(): lax.all_to_all(primal, 'seq', split_axis=3, concat_axis=1, tiled=True)  106 us
    all_to_all x1, waiting for transfers between devices, body(): lax.all_to_all(tangent, 'seq', split_axis=3, concat_axis=1, tiled=True)  94 us
    sub x4, matrix products, block_jvp(): expo = jnp.exp(scores - top)  27.5 us
    unnamed x20, local copies, waits for them, and re-layouts  27.3 us
    all_to_all x1, waiting for transfers between devices, body(): lax.all_to_all(douts, 'seq', split_axis=1, concat_axis=2, tiled=True)  25.9 us
    unnamed x2, other arithmetic  22.2 us
    dot_general x4, matrix products, block_jvp(): jnp.einsum('qhd,khd->hqk', query_block, dkeys, preferred_element_type=jnp...  22 us
    dot_general x4, matrix products, block_jvp(): jnp.einsum('hqk,khd->qhd', dprobs, values, preferred_element_type=jnp.flo...  18.2 us
  transfers between devices with their start and end apart: 6, of which 4 were waited for; matrix products, arithmetic and copies ran while one was open for 38% of the time, Pallas kernels for 0%

commit v1 on v0

--- a/solution.py
+++ b/solution.py
@@ -4,6 +4,12 @@
 from jax.sharding import PartitionSpec as P
 
 HEAD_DIM = 128
+
+
+def swap_blocks(value, axis, split, join):
+    cells = jnp.split(value, lax.axis_size(axis), axis=split)
+    incoming = lax.all_to_all(jnp.stack(cells), axis, 0, 0)
+    return jnp.concatenate(incoming, axis=join)
 
 
 def block_jvp(query_block, dquery_block, keys, dkeys, values, dvalues):
@@ -30,7 +36,7 @@
 def body(primal, tangent, cotangent):
     prim_heads, tang_heads = (
         lax.all_to_all(primal, "seq", split_axis=3, concat_axis=1, tiled=True),
-        lax.all_to_all(tangent, "seq", split_axis=3, concat_axis=1, tiled=True),
+        swap_blocks(tangent, "seq", 3, 1),
     )
     seq_len = prim_heads.shape[1]
     local_width = prim_heads.shape[3]

time: 480 us -> 457 us (0.952)
  waiting for transfers between devices: 236 us -> 207 us
  local copies, waits for them, and re-layouts: 86.2 us -> 92.4 us
    all_to_all x1, waiting for transfers between devices: 94 us -> 67.7 us  [swap_blocks(): incoming = lax.all_to_all(jnp.stack(cells), axis, 0, 0)]
    unnamed x20 -> x36, local copies, waits for them, and re-layouts: 27.3 us -> 41.6 us
    reshape x1, local copies, waits for them, and re-layouts: 6.36 us -> 0.48 us  [body(): outs = outs.reshape(1, seq_len, local_width)]
where the time goes in v1:
time: 457 us; the launch traced here: 456 us
  waiting for transfers between devices  207 us (45%)
  matrix products  93.8 us (21%)
  local copies, waits for them, and re-layouts  92.4 us (20%)
  starting transfers between devices  25.5 us (6%)
  other arithmetic  22.4 us (5%)
  between operations  14.2 us (3%)
    all_to_all x1, waiting for transfers between devices, body(): lax.all_to_all(primal, 'seq', split_axis=3, concat_axis=1, tiled=True)  103 us
    all_to_all x1, waiting for transfers between devices, swap_blocks(): incoming = lax.all_to_all(jnp.stack(cells), axis, 0, 0)  67.7 us
    unnamed x36, local copies, waits for them, and re-layouts  41.6 us
    sub x4, matrix products, block_jvp(): expo = jnp.exp(scores - top)  27.4 us
    all_to_all x1, waiting for transfers between devices, body(): lax.all_to_all(douts, 'seq', split_axis=1, concat_axis=2, tiled=True)  25.8 us
    unnamed x2, other arithmetic  22.4 us
    dot_general x4, matrix products, block_jvp(): jnp.einsum('qhd,khd->hqk', query_block, dkeys, preferred_element_type=jnp...  21.8 us
    dot_general x4, matrix products, block_jvp(): jnp.einsum('hqk,khd->qhd', dprobs, values, preferred_element_type=jnp.flo...  18.2 us
  transfers between devices with their start and end apart: 6, of which 4 were waited for; matrix products, arithmetic and copies ran while one was open for 38% of the time, Pallas kernels for 0%

profile of v1, /device:TPU:6, one launch (start us, length us, event | category | flops | bytes accessed | tf_op | source)
XLA Modules:
  0.0 455.9 jit_solution(10449963140685899186)
XLA Ops:
  25.9 11.2 %all-to-all-start.1 = ((bf16[16,1,128,3,256]{4,2,3,1,0:T(8,128)(2,1)}), bf16[16,1,128,3,256]{4,2,3,1,0:T(8,128)(2,1)S(1)}, u32[]{:S(2)}, u32[]{:S(2)}) async-start(bf16[16,1,128,3,256]{4,2,3,1,0:T(8,128)(2,1)} %bitcast_dynamic-update-slice_fusion), calls=%async_computation.1 | async-start | bytes 6291456 | tf_op jit(solution)/shard_map/all_to_all | solution.py:11
  37.1 7.2 %copy.39 = bf16[1,128,3,4096]{1,2,0,3:T(4,128)(2,1)} copy(bf16[1,128,3,4096]{3,1,2,0:T(8,128)(2,1)} %param.5) | data formatting | bytes 6291456 | tf_op args[0]
  44.2 67.7 %all-to-all-done.1 = bf16[16,1,128,3,256]{4,2,3,1,0:T(8,128)(2,1)S(1)} async-done(((bf16[16,1,128,3,256]{4,2,3,1,0:T(8,128)(2,1)}), bf16[16,1,128,3,256]{4,2,3,1,0:T(8,128)(2,1)S(1)}, u32[]{:S(2)}, u32[]{:S(2)}) %all-to-all-start.1) | async-done | bytes 3145760 | tf_op jit(solution)/shard_map/all_to_all | solution.py:11
  112.0 4.6 all-to-all-start
  132.7 103.2 %all-to-all-done = bf16[1,128,3,4096]{1,2,0,3:T(4,128)(2,1)} async-done(((bf16[1,128,3,4096]{1,2,0,3:T(4,128)(2,1)}), bf16[1,128,3,4096]{1,2,0,3:T(4,128)(2,1)}, u32[]{:S(2)}, u32[]{:S(2)}) %all-to-all-start) | async-done | bytes 3145760 | tf_op jit(solution)/shard_map/all_to_all | solution.py:38
  235.9 4.8 %copy.78 = bf16[1,128,3,16,256]{1,3,4,2,0:T(8,128)(2,1)S(1)} copy(bf16[1,128,3,16,256]{1,2,4,3,0:T(4,128)(2,1)} %bitcast.6) | data formatting | bytes 6291456 | tf_op jit(solution)/shard_map/all_to_all | solution.py:38
  251.7 98.9 %while.12 = (s32[]{:T(128)}, bf16[4,512,2,128]{3,2,1,0:T(2,128)(2,1)S(1)}, bf16[4,512,2,128]{3,2,1,0:T(2,128)(2,1)}, bf16[4,512,2,128]{3,1,0,2:T(8,128)(2,1)}, b...) while((s32[]{:T(128)}, ...), condition=%wide.region_4.5_spmd, body=%wide.region_0.4_spmd.sunk | while | flops 3255174144 | bytes 131365072 | solution.py:55
  251.7 6.9 %fusion.95 = (f32[2,512]{1,0:T(2,128)S(1)}, f32[2,512,2048]{2,1,0:T(8,128)}) fusion(bf16[2048,2,128]{2,0,1:T(8,128)(2,1)S(1)} %get-tuple-element.213, bf16[4,512,2,128]{3,1,0,2:T(8,128)(2,1)} %get-tuple-element.212, s32[]{:T(128)} %get-tuple-element.199), kind=kOutput, calls=%fused_computation.64.clone.1 | convolution fusion | flops 543164416 | bytes 9703936 | tf_op jit(solution)/shard_map/while/body/eval_jaxpr/sub | solution.py:21
  262.4 5.4 %multiply_reduce_fusion.3 = (f32[2,512]{1,0:T(2,128)S(1)}, f32[2,512,2048]{2,1,0:T(8,128)}) fusion(f32[2,512,2048]{2,1,0:T(8,128)S(1)} %copy-done.8, f32[2,512]{1,0:T(2,128)S(1)} %get-tuple-element.184, f32[2,512,2048]{2,1,0:T(8,128)S(1)} %fusion.96, bf16[2048,2,128]{2,0,1:T(8,128)(2,1)S(1)} %copy-done.6, ...), kind=kOutput, calls=%fused_computation.2.clone.1 | convolution fusion | flops 547355648 | bytes 26485248 | tf_op jit(solution)/shard_map/while/body/eval_jaxpr/qhd,khd->hqk/dot_general | solution.py:27
  276.4 6.9 %fusion.95 = (f32[2,512]{1,0:T(2,128)S(1)}, f32[2,512,2048]{2,1,0:T(8,128)}) fusion(bf16[2048,2,128]{2,0,1:T(8,128)(2,1)S(1)} %get-tuple-element.213, bf16[4,512,2,128]{3,1,0,2:T(8,128)(2,1)} %get-tuple-element.212, s32[]{:T(128)} %get-tuple-element.199), kind=kOutput, calls=%fused_computation.64.clone.1 | convolution fusion | flops 543164416 | bytes 9703936 | tf_op jit(solution)/shard_map/while/body/eval_jaxpr/sub | solution.py:21
  287.0 5.5 %multiply_reduce_fusion.3 = (f32[2,512]{1,0:T(2,128)S(1)}, f32[2,512,2048]{2,1,0:T(8,128)}) fusion(f32[2,512,2048]{2,1,0:T(8,128)S(1)} %copy-done.8, f32[2,512]{1,0:T(2,128)S(1)} %get-tuple-element.184, f32[2,512,2048]{2,1,0:T(8,128)S(1)} %fusion.96, bf16[2048,2,128]{2,0,1:T(8,128)(2,1)S(1)} %copy-done.6, ...), kind=kOutput, calls=%fused_computation.2.clone.1 | convolution fusion | flops 547355648 | bytes 26485248 | tf_op jit(solution)/shard_map/while/body/eval_jaxpr/qhd,khd->hqk/dot_general | solution.py:27
  301.0 6.9 %fusion.95 = (f32[2,512]{1,0:T(2,128)S(1)}, f32[2,512,2048]{2,1,0:T(8,128)}) fusion(bf16[2048,2,128]{2,0,1:T(8,128)(2,1)S(1)} %get-tuple-element.213, bf16[4,512,2,128]{3,1,0,2:T(8,128)(2,1)} %get-tuple-element.212, s32[]{:T(128)} %get-tuple-element.199), kind=kOutput, calls=%fused_computation.64.clone.1 | convolution fusion | flops 543164416 | bytes 9703936 | tf_op jit(solution)/shard_map/while/body/eval_jaxpr/sub | solution.py:21
  311.7 5.5 %multiply_reduce_fusion.3 = (f32[2,512]{1,0:T(2,128)S(1)}, f32[2,512,2048]{2,1,0:T(8,128)}) fusion(f32[2,512,2048]{2,1,0:T(8,128)S(1)} %copy-done.8, f32[2,512]{1,0:T(2,128)S(1)} %get-tuple-element.184, f32[2,512,2048]{2,1,0:T(8,128)S(1)} %fusion.96, bf16[2048,2,128]{2,0,1:T(8,128)(2,1)S(1)} %copy-done.6, ...), kind=kOutput, calls=%fused_computation.2.clone.1 | convolution fusion | flops 547355648 | bytes 26485248 | tf_op jit(solution)/shard_map/while/body/eval_jaxpr/qhd,khd->hqk/dot_general | solution.py:27
  317.2 4.6 %fusion.97 = f32[2,512,128]{2,1,0:T(8,128)S(1)} fusion(bf16[2048,2,128]{2,0,1:T(8,128)(2,1)S(1)} %copy-done.7, f32[2,512,2048]{2,1,0:T(8,128)} %get-tuple-element.185, f32[2,512]{1,0:T(2,128)S(1)} %get-tuple-element.186, f32[2,512,2048]{2,1,0:T(8,128)S(1)} %copy-done.8, f32[2,512]{1,0:T(2,128)S(1)} %get-tuple-element.184), kind=kOutput, calls=%fused_computation.7.clone.1 | convolution fusion | flops 545259520 | bytes 18358272 | tf_op jit(solution)/shard_map/while/body/eval_jaxpr/hqk,khd->qhd/dot_general | solution.py:32
  325.8 6.9 %fusion.95 = (f32[2,512]{1,0:T(2,128)S(1)}, f32[2,512,2048]{2,1,0:T(8,128)}) fusion(bf16[2048,2,128]{2,0,1:T(8,128)(2,1)S(1)} %get-tuple-element.213, bf16[4,512,2,128]{3,1,0,2:T(8,128)(2,1)} %get-tuple-element.212, s32[]{:T(128)} %get-tuple-element.199), kind=kOutput, calls=%fused_computation.64.clone.1 | convolution fusion | flops 543164416 | bytes 9703936 | tf_op jit(solution)/shard_map/while/body/eval_jaxpr/sub | solution.py:21
  336.6 5.4 %multiply_reduce_fusion.3 = (f32[2,512]{1,0:T(2,128)S(1)}, f32[2,512,2048]{2,1,0:T(8,128)}) fusion(f32[2,512,2048]{2,1,0:T(8,128)S(1)} %copy-done.8, f32[2,512]{1,0:T(2,128)S(1)} %get-tuple-element.184, f32[2,512,2048]{2,1,0:T(8,128)S(1)} %fusion.96, bf16[2048,2,128]{2,0,1:T(8,128)(2,1)S(1)} %copy-done.6, ...), kind=kOutput, calls=%fused_computation.2.clone.1 | convolution fusion | flops 547355648 | bytes 26485248 | tf_op jit(solution)/shard_map/while/body/eval_jaxpr/qhd,khd->hqk/dot_general | solution.py:27
  351.5 6.0 %fusion.53 = f32[2560,256]{0,1:T(8,128)S(1)} fusion(bf16[1,2048,2560]{2,1,0:T(8,128)(2,1)} %all-gather.2.cloned.1.call-done, bf16[256,8,2,128]{3,2,1,0:T(2,128)(2,1)} %bitcast.145), kind=kOutput, calls=%fused_computation.40 | convolution fusion | flops 2684354560 | bytes 14155776 | tf_op jit(solution)/shard_map/dot_general | solution.py:64
  361.9 10.8 %reduce = bf16[2048,256]{1,0:T(8,128)(2,1)S(1)} reduce(bf16[2048,1,256]{2,1,0:T(2,128)(2,1)S(1)} %bitcast.143, bf16[]{:T(256)} %broadcast.18), dimensions={1}, to_apply=%bitcast.100.reduce_sub_computation | reduce | bytes 2097154
  373.8 4.9 %all-to-all-start.2 = ((bf16[16,2,16384]{2,1,0:T(2,128)(2,1)}), bf16[16,2,16384]{2,1,0:T(2,128)(2,1)S(1)}, u32[]{:S(2)}, u32[]{:S(2)}) async-start(bf16[16,2,16384]{2,1,0:T(2,128)(2,1)} %reshape.22), calls=%async_computation.2 | async-start | bytes 2097152 | tf_op jit(solution)/shard_map/all_to_all | solution.py:59
  378.7 6.4 %reshape.19 = bf16[1,2048,256]{2,0,1:T(2,128)(2,1)S(1)} reshape(bf16[4,512,2,128]{3,2,1,0:T(2,128)(2,1)} %get-tuple-element.52) | data formatting | bytes 2097152 | tf_op jit(solution)/shard_map/reshape | solution.py:57
  385.1 11.6 %reduce.1 = bf16[2048,256]{1,0:T(8,128)(2,1)} reduce(bf16[2048,1,256]{2,1,0:T(2,128)(2,1)S(1)} %bitcast.144, bf16[]{:T(256)} %broadcast.18), dimensions={1}, to_apply=%bitcast.102.reduce_sub_computation | reduce | bytes 2097154
  398.8 9.9 %all-to-all-done.2 = bf16[16,2,16384]{2,1,0:T(2,128)(2,1)S(1)} async-done(((bf16[16,2,16384]{2,1,0:T(2,128)(2,1)}), bf16[16,2,16384]{2,1,0:T(2,128)(2,1)S(1)}, u32[]{:S(2)}, u32[]{:S(2)}) %all-to-all-start.2) | async-done | bytes 1048608 | tf_op jit(solution)/shard_map/all_to_all | solution.py:59
  408.7 4.8 %all-to-all-start.3 = ((bf16[16,2,16384]{2,1,0:T(2,128)(2,1)}), bf16[16,2,16384]{2,1,0:T(2,128)(2,1)}, u32[]{:S(2)}, u32[]{:S(2)}) async-start(bf16[16,2,16384]{2,1,0:T(2,128)(2,1)} %reshape.24), calls=%async_computation.3 | async-start | bytes 2097152 | tf_op jit(solution)/shard_map/all_to_all | solution.py:60
  416.7 25.8 %all-to-all-done.3 = bf16[16,2,16384]{2,1,0:T(2,128)(2,1)} async-done(((bf16[16,2,16384]{2,1,0:T(2,128)(2,1)}), bf16[16,2,16384]{2,1,0:T(2,128)(2,1)}, u32[]{:S(2)}, u32[]{:S(2)}) %all-to-all-start.3) | async-done | bytes 1048608 | tf_op jit(solution)/shard_map/all_to_all | solution.py:60
  (109 shorter events, 108.9 us)
Async XLA Ops:
  7.2 13.1 %copy-start.4 = (bf16[1,128,3,4096]{3,1,2,0:T(8,128)(2,1)S(1)}, bf16[1,128,3,4096]{3,1,2,0:T(8,128)(2,1)}, u32[]{:S(2)}) copy-start(bf16[1,128,3,4096]{3,1,2,0:T(8,128)(2,1)} %param.6) | copy-start | bytes 9437188
  25.9 86.1 %all-to-all-start.1 = ((bf16[16,1,128,3,256]{4,2,3,1,0:T(8,128)(2,1)}), bf16[16,1,128,3,256]{4,2,3,1,0:T(8,128)(2,1)S(1)}, u32[]{:S(2)}, u32[]{:S(2)}) async-start(bf16[16,1,128,3,256]{4,2,3,1,0:T(8,128)(2,1)} %bitcast_dynamic-update-slice_fusion), calls=%async_computation.1 | async-start | bytes 6291456 | tf_op jit(solution)/shard_map/all_to_all | solution.py:11
  112.0 124.0 %all-to-all-start = ((bf16[1,128,3,4096]{1,2,0,3:T(4,128)(2,1)}), bf16[1,128,3,4096]{1,2,0,3:T(4,128)(2,1)}, u32[]{:S(2)}, u32[]{:S(2)}) async-start(bf16[1,128,3,4096]{1,2,0,3:T(4,128)(2,1)} %copy.39), calls=%async_computation | async-start | bytes 8388608 | tf_op jit(solution)/shard_map/all_to_all | solution.py:38
  116.5 234.0 %all-gather.2.cloned.1.call-start = ((), (), s32[]{:S(2)}) async-start(), calls=%async_computation.5 | async-start | bytes 11141120 | tf_op jit(solution)/shard_map/all_gather | solution.py:62
  117.3 331.8 %reduce-scatter.4.cloned.1.call-start = ((), (), s32[]{:S(2)}) async-start(), calls=%async_computation.6 | async-start | bytes 2785280
  126.8 4.6 %copy-start.3 = (bf16[2048,2,128]{0,2,1:T(8,128)(2,1)S(1)}, bf16[2048,2,128]{0,2,1:T(8,128)(2,1)}, u32[]{:S(2)}) copy-start(bf16[2048,2,128]{0,2,1:T(8,128)(2,1)} %get-tuple-element.116) | copy-start | bytes 3145732
  247.5 4.2 copy-start
  258.6 3.8 copy-start.8
  262.4 5.4 %copy-start.7 = (bf16[2048,2,128]{2,0,1:T(8,128)(2,1)S(1)}, bf16[2048,2,128]{2,0,1:T(8,128)(2,1)}, u32[]{:S(2)}) copy-start(bf16[2048,2,128]{2,0,1:T(8,128)(2,1)} %get-tuple-element.214) | copy-start | bytes 3145732 | tf_op jit(solution)/shard_map/while
  267.8 4.6 copy-start.5
  283.2 2.4 copy-start.6
  283.2 3.8 copy-start.8
  287.0 5.5 %copy-start.7 = (bf16[2048,2,128]{2,0,1:T(8,128)(2,1)S(1)}, bf16[2048,2,128]{2,0,1:T(8,128)(2,1)}, u32[]{:S(2)}) copy-start(bf16[2048,2,128]{2,0,1:T(8,128)(2,1)} %get-tuple-element.214) | copy-start | bytes 3145732 | tf_op jit(solution)/shard_map/while
  292.5 4.5 copy-start.5
  307.9 2.4 copy-start.6
  307.9 3.8 copy-start.8
  311.7 5.5 %copy-start.7 = (bf16[2048,2,128]{2,0,1:T(8,128)(2,1)S(1)}, bf16[2048,2,128]{2,0,1:T(8,128)(2,1)}, u32[]{:S(2)}) copy-start(bf16[2048,2,128]{2,0,1:T(8,128)(2,1)} %get-tuple-element.214) | copy-start | bytes 3145732 | tf_op jit(solution)/shard_map/while
  317.2 4.6 %copy-start.5 = (bf16[2048,2,128]{2,0,1:T(8,128)(2,1)S(1)}, bf16[2048,2,128]{2,0,1:T(8,128)(2,1)}, u32[]{:S(2)}) copy-start(bf16[2048,2,128]{2,0,1:T(8,128)(2,1)} %get-tuple-element.215) | copy-start | bytes 3145732 | tf_op jit(solution)/shard_map/while
  332.7 2.4 copy-start.6
  332.7 3.9 copy-start.8
  336.6 5.4 %copy-start.7 = (bf16[2048,2,128]{2,0,1:T(8,128)(2,1)S(1)}, bf16[2048,2,128]{2,0,1:T(8,128)(2,1)}, u32[]{:S(2)}) copy-start(bf16[2048,2,128]{2,0,1:T(8,128)(2,1)} %get-tuple-element.214) | copy-start | bytes 3145732 | tf_op jit(solution)/shard_map/while
  342.0 4.5 copy-start.5
  373.8 34.9 %all-to-all-start.2 = ((bf16[16,2,16384]{2,1,0:T(2,128)(2,1)}), bf16[16,2,16384]{2,1,0:T(2,128)(2,1)S(1)}, u32[]{:S(2)}, u32[]{:S(2)}) async-start(bf16[16,2,16384]{2,1,0:T(2,128)(2,1)} %reshape.22), calls=%async_computation.2 | async-start | bytes 2097152 | tf_op jit(solution)/shard_map/all_to_all | solution.py:59
  408.7 33.8 %all-to-all-start.3 = ((bf16[16,2,16384]{2,1,0:T(2,128)(2,1)}), bf16[16,2,16384]{2,1,0:T(2,128)(2,1)}, u32[]{:S(2)}, u32[]{:S(2)}) async-start(bf16[16,2,16384]{2,1,0:T(2,128)(2,1)} %reshape.24), calls=%async_computation.3 | async-start | bytes 2097152 | tf_op jit(solution)/shard_map/all_to_all | solution.py:60
  (3 other events, 4.6 us)
Sparse Core Ops, SparseCore 0:
  120.0 223.5 all-gather.1
  359.8 61.7 reduce-scatter.3
